TPU v7x, 512 devices: a whole 4x8x8 slice. The times are simulated.
512 devices in a mesh: dp: 32 (over y, x_hi, core), tensor: 16 (over z, x_lo).
Axes of the slice: x: 4 (x_hi: 2, x_lo: 2; x = x_hi * 2 + x_lo), y: 8, z: 8, core: 2. Of those that a mesh axis runs over, the one named last changes fastest.
Arguments:
- tokens: bfloat16 [65536, 896], P(('dp', 'tensor')), parts along dimension 0, may hold values from -6 to 6
- smooth_scale: float32 [896], replicated, may hold values from 0.25 to 4
- gate_weight: bfloat16 [4864, 896], P('tensor'), may hold values from -0.1875 to 0.1875
- up_weight: bfloat16 [4864, 896], P('tensor'), may hold values from -0.1875 to 0.1875
- down_weight: bfloat16 [4864, 896], P('tensor'), may hold values from -0.078125 to 0.078125
Outputs:
- mixed: bfloat16 [65536, 896], P(('dp', 'tensor')), parts along dimension 0
There are 32 independent parts, one for each index of `dp`. A program takes and returns all parts, laid end to end along the dimension named above; an argument that names none is the same for every part. Nothing has to cross between parts.
All inputs are finite; a program needn't handle non-finite values.
Results may differ from a plain program's by a relative error of at most 0.0064.
Values may be sent and summed in bfloat16 or wider, within the bound.
A program may use at most 64 MiB of HBM per device.

v0:
```python
import jax
import jax.numpy as jnp
from jax import lax
from jax.sharding import PartitionSpec as P


def from_behind(block, axis, distance):
    devices = range(lax.axis_size(axis))
    route = [((i - distance) % len(devices), i) for i in devices]
    return lax.ppermute(block, axis, route)


def shards(tokens, smooth_scale, gate_weight, up_weight, down_weight):
    smoothed = (tokens.astype(jnp.float32) / smooth_scale[None, :]).astype(jnp.bfloat16)
    row_count = tokens.shape[0]
    contract = (((1,), (1,)), ((), ()))
    row_piece = lax.all_gather(smoothed, "tensor", axis=0, tiled=True)
    gate_out = lax.dot_general(row_piece, gate_weight, contract, preferred_element_type=jnp.float32)
    up_out = lax.dot_general(row_piece, up_weight, contract, preferred_element_type=jnp.float32)
    hidden = (jax.nn.silu(gate_out) * up_out).astype(jnp.bfloat16)
    devices_n = lax.axis_size("tensor")
    position = lax.axis_index("tensor")

    def partial_for(block_index):
        block_start = (block_index + 2 * devices_n) % devices_n * row_count
        block_rows = lax.dynamic_slice_in_dim(hidden, block_start, row_count, 0)
        return jnp.dot(block_rows, down_weight, preferred_element_type=jnp.float32)

    def forward_hop(hop_index, carried):
        moved = from_behind(carried, "tensor", 1)
        return moved + partial_for(position - 1 - hop_index)

    summed = lax.fori_loop(1, devices_n, forward_hop, partial_for(position - 1))
    return summed.astype(jnp.bfloat16)


def solution(mesh):
    return jax.shard_map(
        shards,
        mesh=mesh,
        in_specs=(
            P(("dp", "tensor"), None),
            P(),
            P("tensor", None),
            P("tensor", None),
            P("tensor", None),
        ),
        out_specs=P(("dp", "tensor"), None),
        check_vma=False,
    )
```

profile of v0, /device:TPU:56, one launch (start us, length us, event | category | flops | bytes accessed | tf_op | source)
XLA Modules:
  0.0 338.1 jit_solution(13841516995008854079)
XLA Ops:
  6.5 0.0 copy-start
  6.5 0.0 all-gather.2.cloned.1.call-start
  6.5 1.7 divide_convert_fusion
  8.3 0.0 all-gather.2.cloned.1.call-update
  8.3 0.0 copy-start.3
  8.3 100.4 %all-gather.2.cloned.1.call-done = bf16[2048,896]{1,0:T(8,128)(2,1)} async-done(((bf16[128,896]{1,0:T(8,128)(2,1)}), bf16[2048,896]{1,0:T(8,128)(2,1)}) %all-gather.2.cloned.1.call-update) | async-done | bytes 3670032 | tf_op jit(solution)/shard_map/all_gather | solution.py:17
  108.7 0.0 copy-done
  108.7 0.0 copy-start.2
  108.7 3.7 %fusion.6 = f32[2048,304]{0,1:T(8,128)S(1)} fusion(bf16[2048,896]{1,0:T(8,128)(2,1)} %all-gather.2.cloned.1.call-done, bf16[304,896]{1,0:T(8,128)(2,1)S(1)} %copy-done), kind=kOutput, calls=%fused_computation.9 | convolution fusion | flops 1115684864 | bytes 6705152 | tf_op jit(solution)/shard_map/dot_general | solution.py:18
  112.4 0.0 copy-done.3
  112.4 0.0 copy-done.2
  112.4 0.0 copy-start.1
  112.4 1.6 fusion.2
  114.0 0.0 copy-done.1
  114.1 0.3 fusion.3
  114.4 216.2 %while.15 = (s32[]{:T(128)}, f32[128,896]{1,0:T(8,128)S(1)}, s32[]{:T(128)}, bf16[2048,304]{0,1:T(8,128)(2,1)S(1)}, bf16[304,896]{1,0:T(8,128)(2,1)S(1)}, /*inde...) while((s32[]{:T(128)}, f32[128,896]{1,0:T(8,128)S(1)}, ...), condition=%wide.region_1.2_spmd, body=%wide.region_0.1_spmd.sunk | while | flops 69845008 | bytes 3375444 | solution.py:33
  114.4 1.9 collective-permute-start
  116.4 10.5 %collective-permute-done = f32[128,896]{1,0:T(8,128)S(1)} collective-permute-done((f32[128,896]{1,0:T(8,128)S(1)}, f32[128,896]{1,0:T(8,128)S(1)}, u32[]{:S(2)}, u32[]{:S(2)}) %collective-permute-start) | collective-permute-done | bytes 458784 | tf_op jit(solution)/shard_map/while/body/eval_jaxpr/ppermute | solution.py:10
  126.9 0.3 convolution_add_fusion.2
  127.2 1.9 collective-permute-start
  129.2 10.5 %collective-permute-done = f32[128,896]{1,0:T(8,128)S(1)} collective-permute-done((f32[128,896]{1,0:T(8,128)S(1)}, f32[128,896]{1,0:T(8,128)S(1)}, u32[]{:S(2)}, u32[]{:S(2)}) %collective-permute-start) | collective-permute-done | bytes 458784 | tf_op jit(solution)/shard_map/while/body/eval_jaxpr/ppermute | solution.py:10
  139.7 0.3 convolution_add_fusion.2
  140.1 1.9 collective-permute-start
  142.0 11.4 %collective-permute-done = f32[128,896]{1,0:T(8,128)S(1)} collective-permute-done((f32[128,896]{1,0:T(8,128)S(1)}, f32[128,896]{1,0:T(8,128)S(1)}, u32[]{:S(2)}, u32[]{:S(2)}) %collective-permute-start) | collective-permute-done | bytes 458784 | tf_op jit(solution)/shard_map/while/body/eval_jaxpr/ppermute | solution.py:10
  153.4 0.3 convolution_add_fusion.2
  153.8 1.9 collective-permute-start
  155.7 12.5 %collective-permute-done = f32[128,896]{1,0:T(8,128)S(1)} collective-permute-done((f32[128,896]{1,0:T(8,128)S(1)}, f32[128,896]{1,0:T(8,128)S(1)}, u32[]{:S(2)}, u32[]{:S(2)}) %collective-permute-start) | collective-permute-done | bytes 458784 | tf_op jit(solution)/shard_map/while/body/eval_jaxpr/ppermute | solution.py:10
  168.2 0.3 convolution_add_fusion.2
  168.6 1.9 collective-permute-start
  170.5 13.6 %collective-permute-done = f32[128,896]{1,0:T(8,128)S(1)} collective-permute-done((f32[128,896]{1,0:T(8,128)S(1)}, f32[128,896]{1,0:T(8,128)S(1)}, u32[]{:S(2)}, u32[]{:S(2)}) %collective-permute-start) | collective-permute-done | bytes 458784 | tf_op jit(solution)/shard_map/while/body/eval_jaxpr/ppermute | solution.py:10
  184.1 0.3 convolution_add_fusion.2
  184.4 1.9 collective-permute-start
  186.4 14.8 %collective-permute-done = f32[128,896]{1,0:T(8,128)S(1)} collective-permute-done((f32[128,896]{1,0:T(8,128)S(1)}, f32[128,896]{1,0:T(8,128)S(1)}, u32[]{:S(2)}, u32[]{:S(2)}) %collective-permute-start) | collective-permute-done | bytes 458784 | tf_op jit(solution)/shard_map/while/body/eval_jaxpr/ppermute | solution.py:10
  201.2 0.3 convolution_add_fusion.2
  201.5 1.9 collective-permute-start
  203.5 15.0 %collective-permute-done = f32[128,896]{1,0:T(8,128)S(1)} collective-permute-done((f32[128,896]{1,0:T(8,128)S(1)}, f32[128,896]{1,0:T(8,128)S(1)}, u32[]{:S(2)}, u32[]{:S(2)}) %collective-permute-start) | collective-permute-done | bytes 458784 | tf_op jit(solution)/shard_map/while/body/eval_jaxpr/ppermute | solution.py:10
  218.4 0.3 convolution_add_fusion.2
  218.8 1.9 collective-permute-start
  220.7 14.2 %collective-permute-done = f32[128,896]{1,0:T(8,128)S(1)} collective-permute-done((f32[128,896]{1,0:T(8,128)S(1)}, f32[128,896]{1,0:T(8,128)S(1)}, u32[]{:S(2)}, u32[]{:S(2)}) %collective-permute-start) | collective-permute-done | bytes 458784 | tf_op jit(solution)/shard_map/while/body/eval_jaxpr/ppermute | solution.py:10
  234.9 0.3 convolution_add_fusion.2
  235.2 1.9 collective-permute-start
  237.2 13.3 %collective-permute-done = f32[128,896]{1,0:T(8,128)S(1)} collective-permute-done((f32[128,896]{1,0:T(8,128)S(1)}, f32[128,896]{1,0:T(8,128)S(1)}, u32[]{:S(2)}, u32[]{:S(2)}) %collective-permute-start) | collective-permute-done | bytes 458784 | tf_op jit(solution)/shard_map/while/body/eval_jaxpr/ppermute | solution.py:10
  250.5 0.3 convolution_add_fusion.2
  250.8 1.9 collective-permute-start
  252.8 12.4 %collective-permute-done = f32[128,896]{1,0:T(8,128)S(1)} collective-permute-done((f32[128,896]{1,0:T(8,128)S(1)}, f32[128,896]{1,0:T(8,128)S(1)}, u32[]{:S(2)}, u32[]{:S(2)}) %collective-permute-start) | collective-permute-done | bytes 458784 | tf_op jit(solution)/shard_map/while/body/eval_jaxpr/ppermute | solution.py:10
  265.2 0.3 convolution_add_fusion.2
  265.5 1.9 collective-permute-start
  267.5 11.5 %collective-permute-done = f32[128,896]{1,0:T(8,128)S(1)} collective-permute-done((f32[128,896]{1,0:T(8,128)S(1)}, f32[128,896]{1,0:T(8,128)S(1)}, u32[]{:S(2)}, u32[]{:S(2)}) %collective-permute-start) | collective-permute-done | bytes 458784 | tf_op jit(solution)/shard_map/while/body/eval_jaxpr/ppermute | solution.py:10
  278.9 0.3 convolution_add_fusion.2
  279.3 1.9 collective-permute-start
  281.2 10.5 %collective-permute-done = f32[128,896]{1,0:T(8,128)S(1)} collective-permute-done((f32[128,896]{1,0:T(8,128)S(1)}, f32[128,896]{1,0:T(8,128)S(1)}, u32[]{:S(2)}, u32[]{:S(2)}) %collective-permute-start) | collective-permute-done | bytes 458784 | tf_op jit(solution)/shard_map/while/body/eval_jaxpr/ppermute | solution.py:10
  291.8 0.3 convolution_add_fusion.2
  292.1 1.9 collective-permute-start
  294.1 10.5 %collective-permute-done = f32[128,896]{1,0:T(8,128)S(1)} collective-permute-done((f32[128,896]{1,0:T(8,128)S(1)}, f32[128,896]{1,0:T(8,128)S(1)}, u32[]{:S(2)}, u32[]{:S(2)}) %collective-permute-start) | collective-permute-done | bytes 458784 | tf_op jit(solution)/shard_map/while/body/eval_jaxpr/ppermute | solution.py:10
  304.6 0.3 convolution_add_fusion.2
  304.9 1.9 collective-permute-start
  306.9 10.5 %collective-permute-done = f32[128,896]{1,0:T(8,128)S(1)} collective-permute-done((f32[128,896]{1,0:T(8,128)S(1)}, f32[128,896]{1,0:T(8,128)S(1)}, u32[]{:S(2)}, u32[]{:S(2)}) %collective-permute-start) | collective-permute-done | bytes 458784 | tf_op jit(solution)/shard_map/while/body/eval_jaxpr/ppermute | solution.py:10
  317.4 0.3 convolution_add_fusion.2
  317.8 1.9 collective-permute-start
  319.7 10.5 %collective-permute-done = f32[128,896]{1,0:T(8,128)S(1)} collective-permute-done((f32[128,896]{1,0:T(8,128)S(1)}, f32[128,896]{1,0:T(8,128)S(1)}, u32[]{:S(2)}, u32[]{:S(2)}) %collective-permute-start) | collective-permute-done | bytes 458784 | tf_op jit(solution)/shard_map/while/body/eval_jaxpr/ppermute | solution.py:10
  330.2 0.3 convolution_add_fusion.2
  330.6 0.7 convert_element_type.15
Async XLA Ops:
  6.5 102.2 %copy-start = (bf16[304,896]{1,0:T(8,128)(2,1)S(1)}, bf16[304,896]{1,0:T(8,128)(2,1)}, u32[]{:S(2)}) copy-start(bf16[304,896]{1,0:T(8,128)(2,1)} %param.9) | copy-start | bytes 1634308
  6.5 102.2 %all-gather.2.cloned.1.call-start = ((), (), s32[]{:S(2)}) async-start(), calls=%async_computation | async-start | bytes 3899392 | tf_op jit(solution)/shard_map/all_gather | solution.py:17
  8.3 104.1 %copy-start.3 = (bf16[304,896]{1,0:T(8,128)(2,1)S(1)}, bf16[304,896]{1,0:T(8,128)(2,1)}, u32[]{:S(2)}) copy-start(bf16[304,896]{1,0:T(8,128)(2,1)} %param.10) | copy-start | bytes 1634308
  108.7 3.7 %copy-start.2 = (bf16[2048,896]{1,0:T(8,128)(2,1)S(1)}, bf16[2048,896]{1,0:T(8,128)(2,1)}, u32[]{:S(2)}) copy-start(bf16[2048,896]{1,0:T(8,128)(2,1)} %all-gather.2.cloned.1.call-done) | copy-start | bytes 11010052
  112.4 1.6 copy-start.1
  114.4 12.5 %collective-permute-start = (f32[128,896]{1,0:T(8,128)S(1)}, f32[128,896]{1,0:T(8,128)S(1)}, u32[]{:S(2)}, u32[]{:S(2)}) collective-permute-start(f32[128,896]{1,0:T(8,128)S(1)} %get-tuple-element.201), channel_id=1, source_target_pairs={{15,0},{0,1},{1,2},{2,3},{3,4},{4,5},{5,6},{6,7},{7,8},{8,9},{9,10... | collective-permute-start | bytes 1376264 | tf_op jit(solution)/shard_map/while/body/eval_jaxpr/ppermute | solution.py:10
  127.2 12.5 %collective-permute-start = (f32[128,896]{1,0:T(8,128)S(1)}, f32[128,896]{1,0:T(8,128)S(1)}, u32[]{:S(2)}, u32[]{:S(2)}) collective-permute-start(f32[128,896]{1,0:T(8,128)S(1)} %get-tuple-element.201), channel_id=1, source_target_pairs={{15,0},{0,1},{1,2},{2,3},{3,4},{4,5},{5,6},{6,7},{7,8},{8,9},{9,10... | collective-permute-start | bytes 1376264 | tf_op jit(solution)/shard_map/while/body/eval_jaxpr/ppermute | solution.py:10
  140.1 13.4 %collective-permute-start = (f32[128,896]{1,0:T(8,128)S(1)}, f32[128,896]{1,0:T(8,128)S(1)}, u32[]{:S(2)}, u32[]{:S(2)}) collective-permute-start(f32[128,896]{1,0:T(8,128)S(1)} %get-tuple-element.201), channel_id=1, source_target_pairs={{15,0},{0,1},{1,2},{2,3},{3,4},{4,5},{5,6},{6,7},{7,8},{8,9},{9,10... | collective-permute-start | bytes 1376264 | tf_op jit(solution)/shard_map/while/body/eval_jaxpr/ppermute | solution.py:10
  153.8 14.4 %collective-permute-start = (f32[128,896]{1,0:T(8,128)S(1)}, f32[128,896]{1,0:T(8,128)S(1)}, u32[]{:S(2)}, u32[]{:S(2)}) collective-permute-start(f32[128,896]{1,0:T(8,128)S(1)} %get-tuple-element.201), channel_id=1, source_target_pairs={{15,0},{0,1},{1,2},{2,3},{3,4},{4,5},{5,6},{6,7},{7,8},{8,9},{9,10... | collective-permute-start | bytes 1376264 | tf_op jit(solution)/shard_map/while/body/eval_jaxpr/ppermute | solution.py:10
  168.6 15.5 %collective-permute-start = (f32[128,896]{1,0:T(8,128)S(1)}, f32[128,896]{1,0:T(8,128)S(1)}, u32[]{:S(2)}, u32[]{:S(2)}) collective-permute-start(f32[128,896]{1,0:T(8,128)S(1)} %get-tuple-element.201), channel_id=1, source_target_pairs={{15,0},{0,1},{1,2},{2,3},{3,4},{4,5},{5,6},{6,7},{7,8},{8,9},{9,10... | collective-permute-start | bytes 1376264 | tf_op jit(solution)/shard_map/while/body/eval_jaxpr/ppermute | solution.py:10
  184.4 16.7 %collective-permute-start = (f32[128,896]{1,0:T(8,128)S(1)}, f32[128,896]{1,0:T(8,128)S(1)}, u32[]{:S(2)}, u32[]{:S(2)}) collective-permute-start(f32[128,896]{1,0:T(8,128)S(1)} %get-tuple-element.201), channel_id=1, source_target_pairs={{15,0},{0,1},{1,2},{2,3},{3,4},{4,5},{5,6},{6,7},{7,8},{8,9},{9,10... | collective-permute-start | bytes 1376264 | tf_op jit(solution)/shard_map/while/body/eval_jaxpr/ppermute | solution.py:10
  201.5 16.9 %collective-permute-start = (f32[128,896]{1,0:T(8,128)S(1)}, f32[128,896]{1,0:T(8,128)S(1)}, u32[]{:S(2)}, u32[]{:S(2)}) collective-permute-start(f32[128,896]{1,0:T(8,128)S(1)} %get-tuple-element.201), channel_id=1, source_target_pairs={{15,0},{0,1},{1,2},{2,3},{3,4},{4,5},{5,6},{6,7},{7,8},{8,9},{9,10... | collective-permute-start | bytes 1376264 | tf_op jit(solution)/shard_map/while/body/eval_jaxpr/ppermute | solution.py:10
  218.8 16.1 %collective-permute-start = (f32[128,896]{1,0:T(8,128)S(1)}, f32[128,896]{1,0:T(8,128)S(1)}, u32[]{:S(2)}, u32[]{:S(2)}) collective-permute-start(f32[128,896]{1,0:T(8,128)S(1)} %get-tuple-element.201), channel_id=1, source_target_pairs={{15,0},{0,1},{1,2},{2,3},{3,4},{4,5},{5,6},{6,7},{7,8},{8,9},{9,10... | collective-permute-start | bytes 1376264 | tf_op jit(solution)/shard_map/while/body/eval_jaxpr/ppermute | solution.py:10
  235.2 15.3 %collective-permute-start = (f32[128,896]{1,0:T(8,128)S(1)}, f32[128,896]{1,0:T(8,128)S(1)}, u32[]{:S(2)}, u32[]{:S(2)}) collective-permute-start(f32[128,896]{1,0:T(8,128)S(1)} %get-tuple-element.201), channel_id=1, source_target_pairs={{15,0},{0,1},{1,2},{2,3},{3,4},{4,5},{5,6},{6,7},{7,8},{8,9},{9,10... | collective-permute-start | bytes 1376264 | tf_op jit(solution)/shard_map/while/body/eval_jaxpr/ppermute | solution.py:10
  250.8 14.3 %collective-permute-start = (f32[128,896]{1,0:T(8,128)S(1)}, f32[128,896]{1,0:T(8,128)S(1)}, u32[]{:S(2)}, u32[]{:S(2)}) collective-permute-start(f32[128,896]{1,0:T(8,128)S(1)} %get-tuple-element.201), channel_id=1, source_target_pairs={{15,0},{0,1},{1,2},{2,3},{3,4},{4,5},{5,6},{6,7},{7,8},{8,9},{9,10... | collective-permute-start | bytes 1376264 | tf_op jit(solution)/shard_map/while/body/eval_jaxpr/ppermute | solution.py:10
  265.5 13.4 %collective-permute-start = (f32[128,896]{1,0:T(8,128)S(1)}, f32[128,896]{1,0:T(8,128)S(1)}, u32[]{:S(2)}, u32[]{:S(2)}) collective-permute-start(f32[128,896]{1,0:T(8,128)S(1)} %get-tuple-element.201), channel_id=1, source_target_pairs={{15,0},{0,1},{1,2},{2,3},{3,4},{4,5},{5,6},{6,7},{7,8},{8,9},{9,10... | collective-permute-start | bytes 1376264 | tf_op jit(solution)/shard_map/while/body/eval_jaxpr/ppermute | solution.py:10
  279.3 12.5 %collective-permute-start = (f32[128,896]{1,0:T(8,128)S(1)}, f32[128,896]{1,0:T(8,128)S(1)}, u32[]{:S(2)}, u32[]{:S(2)}) collective-permute-start(f32[128,896]{1,0:T(8,128)S(1)} %get-tuple-element.201), channel_id=1, source_target_pairs={{15,0},{0,1},{1,2},{2,3},{3,4},{4,5},{5,6},{6,7},{7,8},{8,9},{9,10... | collective-permute-start | bytes 1376264 | tf_op jit(solution)/shard_map/while/body/eval_jaxpr/ppermute | solution.py:10
  292.1 12.5 %collective-permute-start = (f32[128,896]{1,0:T(8,128)S(1)}, f32[128,896]{1,0:T(8,128)S(1)}, u32[]{:S(2)}, u32[]{:S(2)}) collective-permute-start(f32[128,896]{1,0:T(8,128)S(1)} %get-tuple-element.201), channel_id=1, source_target_pairs={{15,0},{0,1},{1,2},{2,3},{3,4},{4,5},{5,6},{6,7},{7,8},{8,9},{9,10... | collective-permute-start | bytes 1376264 | tf_op jit(solution)/shard_map/while/body/eval_jaxpr/ppermute | solution.py:10
  304.9 12.5 %collective-permute-start = (f32[128,896]{1,0:T(8,128)S(1)}, f32[128,896]{1,0:T(8,128)S(1)}, u32[]{:S(2)}, u32[]{:S(2)}) collective-permute-start(f32[128,896]{1,0:T(8,128)S(1)} %get-tuple-element.201), channel_id=1, source_target_pairs={{15,0},{0,1},{1,2},{2,3},{3,4},{4,5},{5,6},{6,7},{7,8},{8,9},{9,10... | collective-permute-start | bytes 1376264 | tf_op jit(solution)/shard_map/while/body/eval_jaxpr/ppermute | solution.py:10
  317.8 12.5 %collective-permute-start = (f32[128,896]{1,0:T(8,128)S(1)}, f32[128,896]{1,0:T(8,128)S(1)}, u32[]{:S(2)}, u32[]{:S(2)}) collective-permute-start(f32[128,896]{1,0:T(8,128)S(1)} %get-tuple-element.201), channel_id=1, source_target_pairs={{15,0},{0,1},{1,2},{2,3},{3,4},{4,5},{5,6},{6,7},{7,8},{8,9},{9,10... | collective-permute-start | bytes 1376264 | tf_op jit(solution)/shard_map/while/body/eval_jaxpr/ppermute | solution.py:10
Sparse Core Ops, SparseCore 0:
  9.4 99.2 all-gather.1
where the time goes:
time: 340 us; the launch traced here: 338 us
  waiting for transfers between devices  282 us (83%)
  starting transfers between devices  28.8 us (8%)
  between operations  13.5 us (4%)
  matrix products  10.5 us (3%)
    ppermute x15, waiting for transfers between devices, from_behind(): return lax.ppermute(block, axis, route)  182 us
    all_gather x1, waiting for transfers between devices, shards(): row_piece = lax.all_gather(smoothed, 'tensor', axis=0, tiled=True)  100 us
    ppermute x15, starting transfers between devices, from_behind(): return lax.ppermute(block, axis, route)  28.8 us
  transfers between devices with their start and end apart: 16, of which 16 were waited for; matrix products, arithmetic and copies ran while one was open for 0% of the time, Pallas kernels for 0%

commit v1 on v0

v1 whole, which is shorter than its diff:
```python
import jax
import jax.numpy as jnp
from jax import lax
from jax.experimental import pallas as pl
from jax.experimental.pallas import tpu as pltpu
from jax.sharding import PartitionSpec as P

MESH = pl.DeviceIdType.MESH
BF16, F32 = jnp.bfloat16, jnp.float32
ROWS_BY_COLS = (((1,), (1,)), ((), ()))
UP, DOWN = 0, 1
PIECES = 4


def kernel(
    tokens_ref, scale_ref, gate_ref, up_ref, down_ref, out_ref,
    raw, x, w, acc, sums, came,
    load_sem, ag_send, ag_recv, rs_send, rs_recv, w_send, w_recv, f_send, f_recv,
):
    dp, t = lax.axis_index("dp"), lax.axis_index("tensor")
    core, x_hi = lax.rem(dp, 2), lax.rem(dp // 2, 2)
    other_t = t + 1 - 2 * lax.rem(t, 2)
    towards = ((dp, lax.rem(t + 2, 16)), (dp, lax.rem(t + 14, 16)))
    sibling = (dp + 1 - 2 * core, t)
    partner = (dp + core * (2 - 4 * x_hi), other_t)

    rows = tokens_ref.shape[0]
    part = rows // PIECES
    half = rows // 2
    units = gate_ref.shape[0]
    big = (units // 2 + 15) // 16 * 16
    small = units - big

    loads = [pltpu.make_async_copy(tokens_ref, raw, load_sem.at[0])]
    for i, ref in enumerate((gate_ref, up_ref, down_ref)):
        loads.append(pltpu.make_async_copy(ref, w.at[i, pl.ds(0, units)], load_sem.at[i + 1]))
    for load in loads:
        load.start()

    barrier = pltpu.get_barrier_semaphore()
    for device in (*towards, sibling, partner):
        pl.semaphore_signal(barrier, inc=1, device_id=device, device_id_type=MESH)

    loads[0].wait()
    x[0] = (raw[...].astype(F32) / scale_ref[...]).astype(BF16)
    pl.semaphore_wait(barrier, 4)

    def gather(way, hop, piece):
        here = hop if way == UP else (8 - hop) % 8
        there = hop + 1 if way == UP else 7 - hop
        at = pl.ds(piece * part, part)
        return pltpu.make_async_remote_copy(
            src_ref=x.at[here, at],
            dst_ref=x.at[there, at],
            send_sem=ag_send.at[way, hop, piece],
            recv_sem=ag_recv.at[way, hop, piece],
            device_id=towards[way],
            device_id_type=MESH,
        )

    first = ((2, 3), (0, 1))
    second = ((0, 1), (2, 3))

    def pass_on(hop, piece_of):
        for way in (UP, DOWN):
            if hop:
                gather(way, hop - 1, piece_of(way)).wait_recv()
            gather(way, hop, piece_of(way)).start()

    def from_partner(i):
        which, start, size = ((core, 0, big), (core, big, small), (2, core * small, big))[i]
        return pltpu.make_async_remote_copy(
            src_ref=w.at[which, pl.ds(pl.multiple_of(start, 16), size)],
            dst_ref=w.at[which, pl.ds(pl.multiple_of(start + units, 16), size)],
            send_sem=w_send.at[i],
            recv_sem=w_recv.at[i],
            device_id=partner,
            device_id_type=MESH,
        )

    def hand_on(i):
        which, start, size = ((core, 0, big), (core, big, small), (2, core * big, small))[i]
        at = pl.ds(pl.multiple_of(start + units, 16), size)
        return pltpu.make_async_remote_copy(
            src_ref=w.at[which, at],
            dst_ref=w.at[which, at],
            send_sem=f_send.at[i],
            recv_sem=f_recv.at[i],
            device_id=sibling,
            device_id_type=MESH,
        )

    def arrived_weights(i):
        from_partner(i).wait_recv()
        hand_on(i).start()

    pass_on(0, lambda way: first[way][0])
    pass_on(0, lambda way: first[way][1])
    pass_on(0, lambda way: second[way][0])
    for load in loads[1:]:
        load.wait()
    for i in range(3):
        from_partner(i).start()

    pass_on(1, lambda way: first[way][0])
    pass_on(1, lambda way: first[way][1])
    pass_on(0, lambda way: second[way][1])
    arrived_weights(0)
    pass_on(2, lambda way: first[way][0])
    pass_on(2, lambda way: first[way][1])
    pass_on(1, lambda way: second[way][0])
    arrived_weights(1)
    pass_on(3, lambda way: first[way][0])
    pass_on(3, lambda way: first[way][1])
    pass_on(1, lambda way: second[way][1])
    arrived_weights(2)
    pass_on(2, lambda way: second[way][0])
    pass_on(2, lambda way: second[way][1])
    for i in range(3):
        hand_on(i).wait_recv()

    def work(*blocks):
        tile = jnp.concatenate([x[s, a : a + n] for s, a, n in blocks], axis=0)
        gate = lax.dot_general(tile, w[0], ROWS_BY_COLS, preferred_element_type=F32)
        up = lax.dot_general(tile, w[1], ROWS_BY_COLS, preferred_element_type=F32)
        hidden = (gate / (1.0 + jnp.exp(-gate)) * up).astype(BF16)
        result = jnp.dot(hidden, w[2], preferred_element_type=F32)
        row = 0
        for s, a, n in blocks:
            acc[s, a : a + n] = result[row : row + n]
            row += n

    def reduce(way, step, piece):
        at = pl.ds(piece * part, part)
        return pltpu.make_async_remote_copy(
            src_ref=sums.at[way, step, at],
            dst_ref=came.at[way, step, at],
            send_sem=rs_send.at[way, step, piece],
            recv_sem=rs_recv.at[way, step, piece],
            device_id=towards[way],
            device_id_type=MESH,
        )

    def send_sum(way, step, piece, add):
        slot = 4 + step if way == UP else 4 - step
        at = pl.ds(piece * part, part)
        value = acc[slot, at]
        if add:
            reduce(way, step - 1, piece).wait_recv()
            value = value + came[way, step - 1, at].astype(F32)
        sums[way, step, at] = value.astype(BF16)
        reduce(way, step, piece).start()

    work((0, 0, rows), (1, 0, rows), (7, 0, rows))
    for way in (UP, DOWN):
        for piece in first[way]:
            gather(way, 3, piece).wait_recv()
    work((3, half, half), (4, 0, rows), (5, 0, half))
    for i in (0, 1):
        for way in (UP, DOWN):
            send_sum(way, 0, first[way][i], False)
    for i in (0, 1):
        for way in (UP, DOWN):
            send_sum(way, 1, second[way][i], False)
    for way in (UP, DOWN):
        for piece in second[way]:
            gather(way, 2, piece).wait_recv()
    work((3, 0, half), (5, half, half), (2, 0, rows), (6, 0, rows))
    for i in (0, 1):
        for way in (UP, DOWN):
            send_sum(way, 1, first[way][i], True)
    for step in (2, 3):
        for order in (second, first):
            for i in (0, 1):
                for way in (UP, DOWN):
                    send_sum(way, step, order[way][i], True)
    for order in (second, first):
        for i in (0, 1):
            for way in (UP, DOWN):
                reduce(way, 3, order[way][i]).wait_recv()
    out_ref[...] = (acc[0] + came[UP, 3].astype(F32) + came[DOWN, 3].astype(F32)).astype(BF16)

    for way in (UP, DOWN):
        for hop in range(4):
            for piece in range(PIECES):
                if hop < 3 or piece in first[way]:
                    gather(way, hop, piece).wait_send()
                if hop > 0 or piece in first[way]:
                    reduce(way, hop, piece).wait_send()
    for i in range(3):
        from_partner(i).wait_send()
        hand_on(i).wait_send()


def shards(tokens, smooth_scale, gate_weight, up_weight, down_weight):
    rows, width = tokens.shape
    units = gate_weight.shape[0]
    here = pl.BlockSpec(memory_space=pl.ANY)
    dma = pltpu.SemaphoreType.DMA
    return pl.pallas_call(
        kernel,
        out_shape=jax.ShapeDtypeStruct((rows, width), BF16),
        in_specs=[here, pl.BlockSpec(memory_space=pltpu.VMEM), here, here, here],
        out_specs=pl.BlockSpec(memory_space=pltpu.VMEM),
        scratch_shapes=[
            pltpu.VMEM((rows, width), BF16),
            pltpu.VMEM((8, rows, width), BF16),
            pltpu.VMEM((3, 2 * units, width), BF16),
            pltpu.VMEM((8, rows, width), F32),
            pltpu.VMEM((2, 4, rows, width), BF16),
            pltpu.VMEM((2, 4, rows, width), BF16),
            dma((4,)),
            dma((2, 4, PIECES)),
            dma((2, 4, PIECES)),
            dma((2, 4, PIECES)),
            dma((2, 4, PIECES)),
            dma((3,)),
            dma((3,)),
            dma((3,)),
            dma((3,)),
        ],
        compiler_params=pltpu.CompilerParams(
            collective_id=0, has_side_effects=True, vmem_limit_bytes=48 << 20
        ),
    )(tokens, smooth_scale.reshape(1, width), gate_weight, up_weight, down_weight)


def solution(mesh):
    return jax.shard_map(
        shards,
        mesh=mesh,
        in_specs=(
            P(("dp", "tensor"), None),
            P(),
            P("tensor", None),
            P("tensor", None),
            P("tensor", None),
        ),
        out_specs=P(("dp", "tensor"), None),
        check_vma=False,
    )
```

time: 340 us -> 58.4 us (0.17)
  waiting for transfers between devices: 282 us -> 0 us
  Pallas kernels: 0 us -> 52.6 us
  starting transfers between devices: 28.8 us -> 0 us
  between operations: 13.5 us -> 0.01 us
  matrix products: 10.5 us -> 0 us
  local copies, waits for them, and re-layouts: 0.02 us -> 5.46 us
    ppermute x15 -> x0, waiting for transfers between devices: 182 us -> none  [from_behind(): return lax.ppermute(block, axis, route)]
    all_gather x1 -> x0, waiting for transfers between devices: 100 us -> none  [shards(): row_piece = lax.all_gather(smoothed, 'tensor', axis=0, tiled=True)]
    pallas_call x0 -> x1, Pallas kernels: none -> 52.6 us  [shards(): pl.pallas_call(kernel, out_shape=jax.ShapeDtypeStruct((rows, width), BF16...]
    ppermute x15 -> x0, starting transfers between devices: 28.8 us -> none  [from_behind(): return lax.ppermute(block, axis, route)]
    dot_general x18 -> x0, matrix products: 10.5 us -> none  [the longest x16 5.22 us: partial_for(): return jnp.dot(block_rows, down_weight, preferred_element_type=jnp.float32)]
    unnamed x8 -> x9, local copies, waits for them, and re-layouts: 0.02 us -> 4.77 us
  transfers between devices with their start and end apart: 16 -> 0, of which waited for: 16 -> 0; matrix products, arithmetic and copies ran while one was open for 0% -> 0% of each run, Pallas kernels for 0% -> 0%
where the time goes in v1:
time: 58.4 us; the launch traced here: 58.1 us
  Pallas kernels  52.6 us (90%)
  local copies, waits for them, and re-layouts  5.46 us (9%)
    pallas_call x1, Pallas kernels, shards(): pl.pallas_call(kernel, out_shape=jax.ShapeDtypeStruct((rows, width), BF16...  52.6 us
    unnamed x9, local copies, waits for them, and re-layouts  4.77 us

profile of v1, /device:TPU:56, one launch (start us, length us, event | category | flops | bytes accessed | tf_op | source)
XLA Modules:
  0.0 58.1 jit_solution(8412014325112140892)
XLA Ops:
  0.0 0.7 %reshape.3.scale_ref = f32[1,896]{1,0:T(1,128)S(1)} reshape(f32[896]{0:T(1024)} %param.6) | data formatting | bytes 7168 | tf_op jit(solution)/shard_map/reshape | solution.py:225
  0.7 0.0 copy-start
  0.7 1.0 %copy-done = bf16[304,896]{1,0:T(8,128)(2,1)S(1)} copy-done((bf16[304,896]{1,0:T(8,128)(2,1)S(1)}, bf16[304,896]{1,0:T(8,128)(2,1)}, u32[]{:S(2)}) %copy-start) | copy-done | bytes 544792
  1.7 0.0 copy-start.1
  1.7 1.0 %copy-done.1 = bf16[304,896]{1,0:T(8,128)(2,1)S(1)} copy-done((bf16[304,896]{1,0:T(8,128)(2,1)S(1)}, bf16[304,896]{1,0:T(8,128)(2,1)}, u32[]{:S(2)}) %copy-start.1) | copy-done | bytes 544792
  2.8 0.0 copy-start.2
  2.8 1.0 %copy-done.2 = bf16[304,896]{1,0:T(8,128)(2,1)S(1)} copy-done((bf16[304,896]{1,0:T(8,128)(2,1)S(1)}, bf16[304,896]{1,0:T(8,128)(2,1)}, u32[]{:S(2)}) %copy-start.2) | copy-done | bytes 544792
  3.8 0.0 copy-start.3
  3.8 0.9 %copy-done.3 = bf16[128,896]{1,0:T(8,128)(2,1)S(1)} copy-done((bf16[128,896]{1,0:T(8,128)(2,1)S(1)}, bf16[128,896]{1,0:T(8,128)(2,1)}, u32[]{:S(2)}) %copy-start.3) | copy-done | bytes 229400
  4.8 52.6 %shard_map.55 = bf16[128,896]{1,0:T(8,128)(2,1)S(1)} custom-call(bf16[128,896]{1,0:T(8,128)(2,1)S(1)} %copy-done.3, f32[1,896]{1,0:T(1,128)S(1)} %reshape.3.scale_ref, bf16[304,896]{1,0:T(8,128)(2,1)S(1)} %copy-done, bf16[304,896]{1,0:T(8,128)(2,1)S(1)} %copy-done.1, bf16[304,896]{1,0:T(8,128)(2,1)S(1)} %copy-done.2), custom_call_target="tpu_custom_call" | custom-call | tf_op jit(solution)/shard_map/pallas_call | solution.py:200
  57.4 0.7 %copy.7 = bf16[128,896]{1,0:T(8,128)(2,1)} copy(bf16[128,896]{1,0:T(8,128)(2,1)S(1)} %shard_map.55) | data formatting | bytes 458752
Async XLA Ops:
  0.7 1.0 %copy-start = (bf16[304,896]{1,0:T(8,128)(2,1)S(1)}, bf16[304,896]{1,0:T(8,128)(2,1)}, u32[]{:S(2)}) copy-start(bf16[304,896]{1,0:T(8,128)(2,1)} %gate_ref.1) | copy-start | bytes 1634308
  1.7 1.0 %copy-start.1 = (bf16[304,896]{1,0:T(8,128)(2,1)S(1)}, bf16[304,896]{1,0:T(8,128)(2,1)}, u32[]{:S(2)}) copy-start(bf16[304,896]{1,0:T(8,128)(2,1)} %up_ref.1) | copy-start | bytes 1634308
  2.8 1.0 %copy-start.2 = (bf16[304,896]{1,0:T(8,128)(2,1)S(1)}, bf16[304,896]{1,0:T(8,128)(2,1)}, u32[]{:S(2)}) copy-start(bf16[304,896]{1,0:T(8,128)(2,1)} %down_ref.1) | copy-start | bytes 1634308
  3.8 0.9 %copy-start.3 = (bf16[128,896]{1,0:T(8,128)(2,1)S(1)}, bf16[128,896]{1,0:T(8,128)(2,1)}, u32[]{:S(2)}) copy-start(bf16[128,896]{1,0:T(8,128)(2,1)} %tokens_ref.1) | copy-start | bytes 688132

commit v2 on v1

--- a/solution.py
+++ b/solution.py
@@ -14,7 +14,7 @@
 
 def kernel(
     tokens_ref, scale_ref, gate_ref, up_ref, down_ref, out_ref,
-    raw, x, w, acc, sums, came,
+    raw, scale, x, w, acc, sums, came,
     load_sem, ag_send, ag_recv, rs_send, rs_recv, w_send, w_recv, f_send, f_recv,
 ):
     dp, t = lax.axis_index("dp"), lax.axis_index("tensor")
@@ -31,9 +31,12 @@
     big = (units // 2 + 15) // 16 * 16
     small = units - big
 
-    loads = [pltpu.make_async_copy(tokens_ref, raw, load_sem.at[0])]
+    loads = [
+        pltpu.make_async_copy(tokens_ref, raw, load_sem.at[0]),
+        pltpu.make_async_copy(scale_ref, scale, load_sem.at[1]),
+    ]
     for i, ref in enumerate((gate_ref, up_ref, down_ref)):
-        loads.append(pltpu.make_async_copy(ref, w.at[i, pl.ds(0, units)], load_sem.at[i + 1]))
+        loads.append(pltpu.make_async_copy(ref, w.at[i, pl.ds(0, units)], load_sem.at[i + 2]))
     for load in loads:
         load.start()
 
@@ -42,7 +45,8 @@
         pl.semaphore_signal(barrier, inc=1, device_id=device, device_id_type=MESH)
 
     loads[0].wait()
-    x[0] = (raw[...].astype(F32) / scale_ref[...]).astype(BF16)
+    loads[1].wait()
+    x[0] = (raw[...].astype(F32) / scale[...][None, :]).astype(BF16)
     pl.semaphore_wait(barrier, 4)
 
     def gather(way, hop, piece):
@@ -97,7 +101,7 @@
     pass_on(0, lambda way: first[way][0])
     pass_on(0, lambda way: first[way][1])
     pass_on(0, lambda way: second[way][0])
-    for load in loads[1:]:
+    for load in loads[2:]:
         load.wait()
     for i in range(3):
         from_partner(i).start()
@@ -195,21 +199,22 @@
 def shards(tokens, smooth_scale, gate_weight, up_weight, down_weight):
     rows, width = tokens.shape
     units = gate_weight.shape[0]
-    here = pl.BlockSpec(memory_space=pl.ANY)
+    here = pl.BlockSpec(memory_space=pltpu.HBM)
     dma = pltpu.SemaphoreType.DMA
     return pl.pallas_call(
         kernel,
         out_shape=jax.ShapeDtypeStruct((rows, width), BF16),
-        in_specs=[here, pl.BlockSpec(memory_space=pltpu.VMEM), here, here, here],
+        in_specs=[here] * 5,
         out_specs=pl.BlockSpec(memory_space=pltpu.VMEM),
         scratch_shapes=[
             pltpu.VMEM((rows, width), BF16),
+            pltpu.VMEM((width,), F32),
             pltpu.VMEM((8, rows, width), BF16),
             pltpu.VMEM((3, 2 * units, width), BF16),
             pltpu.VMEM((8, rows, width), F32),
             pltpu.VMEM((2, 4, rows, width), BF16),
             pltpu.VMEM((2, 4, rows, width), BF16),
-            dma((4,)),
+            dma((5,)),
             dma((2, 4, PIECES)),
             dma((2, 4, PIECES)),
             dma((2, 4, PIECES)),
@@ -220,9 +225,9 @@
             dma((3,)),
         ],
         compiler_params=pltpu.CompilerParams(
-            collective_id=0, has_side_effects=True, vmem_limit_bytes=48 << 20
+            collective_id=0, has_side_effects=True, vmem_limit_bytes=60 << 20
         ),
-    )(tokens, smooth_scale.reshape(1, width), gate_weight, up_weight, down_weight)
+    )(tokens, smooth_scale, gate_weight, up_weight, down_weight)
 
 
 def solution(mesh):

time: 58.4 us -> 54.6 us (0.935)
  local copies, waits for them, and re-layouts: 5.46 us -> 1.65 us
    unnamed x9 -> x1, local copies, waits for them, and re-layouts: 4.77 us -> 1.65 us
    reshape x1 -> x0, local copies, waits for them, and re-layouts: 0.69 us -> none  [shards(): smooth_scale.reshape(1, width)]
where the time goes in v2:
time: 54.6 us; the launch traced here: 54.5 us
  Pallas kernels  52.8 us (97%)
  local copies, waits for them, and re-layouts  1.65 us (3%)
    pallas_call x1, Pallas kernels, shards(): pl.pallas_call(kernel, out_shape=jax.ShapeDtypeStruct((rows, width), BF16...  52.8 us
    unnamed x1, local copies, waits for them, and re-layouts  1.65 us

profile of v2, /device:TPU:56, one launch (start us, length us, event | category | flops | bytes accessed | tf_op | source)
XLA Modules:
  0.0 54.5 jit_solution(16442735614733389379)
XLA Ops:
  0.0 52.8 %shard_map.55 = bf16[128,896]{1,0:T(8,128)(2,1)} custom-call(bf16[128,896]{1,0:T(8,128)(2,1)} %tokens_ref.1, f32[896]{0:T(1024)} %scale_ref.1, bf16[304,896]{1,0:T(8,128)(2,1)} %gate_ref.1, bf16[304,896]{1,0:T(8,128)(2,1)} %up_ref.1, bf16[304,896]{1,0:T(8,128)(2,1)} %down_ref.1), custom_call_target="tpu_custom_call" | custom-call | tf_op jit(solution)/shard_map/pallas_call | solution.py:204
  52.8 1.6 %copy.7 = bf16[128,896]{1,0:T(8,128)(2,1)} copy(bf16[128,896]{1,0:T(8,128)(2,1)} %shard_map.55) | data formatting | bytes 458752

commit v3 on v2

--- a/solution.py
+++ b/solution.py
@@ -31,22 +31,24 @@
     big = (units // 2 + 15) // 16 * 16
     small = units - big
 
-    loads = [
-        pltpu.make_async_copy(tokens_ref, raw, load_sem.at[0]),
-        pltpu.make_async_copy(scale_ref, scale, load_sem.at[1]),
-    ]
+    order = (0, 2, 1, 3)
+    loads = [pltpu.make_async_copy(scale_ref, scale, load_sem.at[0])]
+    for i in order:
+        at = pl.ds(i * part, part)
+        loads.append(pltpu.make_async_copy(tokens_ref.at[at], raw.at[at], load_sem.at[1 + i]))
     for i, ref in enumerate((gate_ref, up_ref, down_ref)):
-        loads.append(pltpu.make_async_copy(ref, w.at[i, pl.ds(0, units)], load_sem.at[i + 2]))
-    for load in loads:
-        load.start()
-
+        loads.append(pltpu.make_async_copy(ref, w.at[i, pl.ds(0, units)], load_sem.at[5 + i]))
     barrier = pltpu.get_barrier_semaphore()
     for device in (*towards, sibling, partner):
         pl.semaphore_signal(barrier, inc=1, device_id=device, device_id_type=MESH)
+    for load in loads:
+        load.start()
 
     loads[0].wait()
-    loads[1].wait()
-    x[0] = (raw[...].astype(F32) / scale[...][None, :]).astype(BF16)
+    for i, load in zip(order, loads[1:5], strict=True):
+        load.wait()
+        at = pl.ds(i * part, part)
+        x[0, at] = (raw[at].astype(F32) / scale[...][None, :]).astype(BF16)
     pl.semaphore_wait(barrier, 4)
 
     def gather(way, hop, piece):
@@ -101,7 +103,7 @@
     pass_on(0, lambda way: first[way][0])
     pass_on(0, lambda way: first[way][1])
     pass_on(0, lambda way: second[way][0])
-    for load in loads[2:]:
+    for load in loads[5:]:
         load.wait()
     for i in range(3):
         from_partner(i).start()
@@ -118,8 +120,6 @@
     pass_on(3, lambda way: first[way][1])
     pass_on(1, lambda way: second[way][1])
     arrived_weights(2)
-    pass_on(2, lambda way: second[way][0])
-    pass_on(2, lambda way: second[way][1])
     for i in range(3):
         hand_on(i).wait_recv()
 
@@ -156,9 +156,11 @@
         reduce(way, step, piece).start()
 
     work((0, 0, rows), (1, 0, rows), (7, 0, rows))
+    pass_on(2, lambda way: second[way][0])
     for way in (UP, DOWN):
         for piece in first[way]:
             gather(way, 3, piece).wait_recv()
+    pass_on(2, lambda way: second[way][1])
     work((3, half, half), (4, 0, rows), (5, 0, half))
     for i in (0, 1):
         for way in (UP, DOWN):
@@ -181,8 +183,14 @@
     for order in (second, first):
         for i in (0, 1):
             for way in (UP, DOWN):
-                reduce(way, 3, order[way][i]).wait_recv()
-    out_ref[...] = (acc[0] + came[UP, 3].astype(F32) + came[DOWN, 3].astype(F32)).astype(BF16)
+                piece = order[way][i]
+                at = pl.ds(piece * part, part)
+                reduce(way, 3, piece).wait_recv()
+                value = acc[0, at] + came[way, 3, at].astype(F32)
+                if order is second:
+                    acc[0, at] = value
+                else:
+                    out_ref[at] = value.astype(BF16)
 
     for way in (UP, DOWN):
         for hop in range(4):
@@ -200,10 +208,11 @@
     rows, width = tokens.shape
     units = gate_weight.shape[0]
     here = pl.BlockSpec(memory_space=pltpu.HBM)
+    operands = (tokens, smooth_scale, gate_weight, up_weight, down_weight)
     dma = pltpu.SemaphoreType.DMA
     return pl.pallas_call(
         kernel,
-        out_shape=jax.ShapeDtypeStruct((rows, width), BF16),
+        out_shape=pltpu.VMEM((rows, width), BF16),
         in_specs=[here] * 5,
         out_specs=pl.BlockSpec(memory_space=pltpu.VMEM),
         scratch_shapes=[
@@ -214,7 +223,7 @@
             pltpu.VMEM((8, rows, width), F32),
             pltpu.VMEM((2, 4, rows, width), BF16),
             pltpu.VMEM((2, 4, rows, width), BF16),
-            dma((5,)),
+            dma((8,)),
             dma((2, 4, PIECES)),
             dma((2, 4, PIECES)),
             dma((2, 4, PIECES)),
@@ -225,9 +234,9 @@
             dma((3,)),
         ],
         compiler_params=pltpu.CompilerParams(
-            collective_id=0, has_side_effects=True, vmem_limit_bytes=60 << 20
+            collective_id=0, has_side_effects=True, vmem_limit_bytes=48 << 20
         ),
-    )(tokens, smooth_scale, gate_weight, up_weight, down_weight)
+    )(*(pltpu.with_memory_space_constraint(o, pltpu.HBM) for o in operands))
 
 
 def solution(mesh):

time: 54.6 us -> 51.2 us (0.938)
  Pallas kernels: 52.8 us -> 50.1 us
  local copies, waits for them, and re-layouts: 1.65 us -> 0.69 us
    pallas_call x1, Pallas kernels: 52.8 us -> 50.1 us  [shards(): pl.pallas_call(kernel, out_shape=pltpu.VMEM((rows, width), BF16), in_spec...]
    unnamed x1, local copies, waits for them, and re-layouts: 1.65 us -> 0.69 us
where the time goes in v3:
time: 51.2 us; the launch traced here: 50.8 us
  Pallas kernels  50.1 us (98%)
  local copies, waits for them, and re-layouts  0.69 us (1%)
    pallas_call x1, Pallas kernels, shards(): pl.pallas_call(kernel, out_shape=pltpu.VMEM((rows, width), BF16), in_spec...  50.1 us

profile of v3, /device:TPU:56, one launch (start us, length us, event | category | flops | bytes accessed | tf_op | source)
XLA Modules:
  0.0 50.8 jit_solution(2124530773999350984)
XLA Ops:
  0.0 50.1 %shard_map.55 = bf16[128,896]{1,0:T(8,128)(2,1)S(1)} custom-call(bf16[128,896]{1,0:T(8,128)(2,1)} %tokens_ref.1, f32[896]{0:T(1024)} %scale_ref.1, bf16[304,896]{1,0:T(8,128)(2,1)} %gate_ref.1, bf16[304,896]{1,0:T(8,128)(2,1)} %up_ref.1, bf16[304,896]{1,0:T(8,128)(2,1)} %down_ref.1), custom_call_target="tpu_custom_call" | custom-call | tf_op jit(solution)/shard_map/pallas_call | solution.py:213
  50.1 0.7 %copy.7 = bf16[128,896]{1,0:T(8,128)(2,1)} copy(bf16[128,896]{1,0:T(8,128)(2,1)S(1)} %shard_map.55) | data formatting | bytes 458752

commit v4 on v3

v4 whole, which is shorter than its diff:
```python
import jax
import jax.numpy as jnp
from jax import lax
from jax.experimental import pallas as pl
from jax.experimental.pallas import tpu as pltpu
from jax.sharding import PartitionSpec as P

MESH = pl.DeviceIdType.MESH
BF16, F32 = jnp.bfloat16, jnp.float32
ROWS_BY_COLS = (((1,), (1,)), ((), ()))
UP, DOWN = 0, 1
PIECES = 4


def kernel(
    tokens_ref, scale_ref, gate_ref, up_ref, down_ref, out_ref,
    raw, scale, x, w, acc, sums, came,
    load_sem, ag_send, ag_recv, rs_send, rs_recv, w_load, w_send, w_recv, f_recv,
):
    dp, t = lax.axis_index("dp"), lax.axis_index("tensor")
    core, x_hi = lax.rem(dp, 2), lax.rem(dp // 2, 2)
    other_t = t + 1 - 2 * lax.rem(t, 2)
    towards = ((dp, lax.rem(t + 2, 16)), (dp, lax.rem(t + 14, 16)))
    sibling = (dp + 1 - 2 * core, t)
    partner = (dp + core * (2 - 4 * x_hi), other_t)

    rows = tokens_ref.shape[0]
    part = rows // PIECES
    half = rows // 2
    units = gate_ref.shape[0]
    big = (units // 2 + 15) // 16 * 16
    small = units - big

    loads = [
        pltpu.make_async_copy(scale_ref, scale, load_sem.at[0]),
        pltpu.make_async_copy(tokens_ref, raw, load_sem.at[1]),
    ]
    for i, ref in enumerate((gate_ref, up_ref, down_ref)):
        loads.append(pltpu.make_async_copy(ref, w.at[i, pl.ds(0, units)], w_load))
    own = w.at[:, pl.ds(0, units)]
    barrier = pltpu.get_barrier_semaphore()
    for device in (*towards, sibling, partner):
        pl.semaphore_signal(barrier, inc=1, device_id=device, device_id_type=MESH)
    for load in loads:
        load.start()
    loads[0].wait()
    loads[1].wait()
    x[0] = (raw[...].astype(F32) / scale[...][None, :]).astype(BF16)
    pl.semaphore_wait(barrier, 4)

    far = ((2, 3), (0, 1))
    near = ((0, 1), (2, 3))

    def gather(way, hop, piece):
        here = hop if way == UP else (8 - hop) % 8
        there = hop + 1 if way == UP else 7 - hop
        at = pl.ds(piece * part, part)
        slot = 4 * hop + (far[way] + near[way]).index(piece)
        return pltpu.make_async_remote_copy(
            src_ref=x.at[here, at],
            dst_ref=x.at[there, at],
            send_sem=ag_send,
            recv_sem=ag_recv.at[way, slot],
            device_id=towards[way],
            device_id_type=MESH,
        )

    def pass_on(hop, which, i):
        for way in (UP, DOWN):
            if hop:
                gather(way, hop - 1, which[way][i]).wait_recv()
            gather(way, hop, which[way][i]).start()

    def from_partner(i):
        which, start, size = ((core, 0, big), (core, big, small), (2, core * small, big))[i]
        return pltpu.make_async_remote_copy(
            src_ref=w.at[which, pl.ds(pl.multiple_of(start, 16), size)],
            dst_ref=w.at[which, pl.ds(pl.multiple_of(start + units, 16), size)],
            send_sem=w_send,
            recv_sem=w_recv.at[i],
            device_id=partner,
            device_id_type=MESH,
        )

    def hand_on(i):
        which, start, size = ((core, 0, big), (core, big, small), (2, core * big, small))[i]
        at = pl.ds(pl.multiple_of(start + units, 16), size)
        return pltpu.make_async_remote_copy(
            src_ref=w.at[which, at],
            dst_ref=w.at[which, at],
            send_sem=w_send,
            recv_sem=f_recv.at[i],
            device_id=sibling,
            device_id_type=MESH,
        )

    def arrived_weights(i):
        from_partner(i).wait_recv()
        hand_on(i).start()

    def work(*blocks):
        tile = jnp.concatenate([x[s, a : a + n] for s, a, n in blocks], axis=0)
        gate = lax.dot_general(tile, w[0], ROWS_BY_COLS, preferred_element_type=F32)
        up = lax.dot_general(tile, w[1], ROWS_BY_COLS, preferred_element_type=F32)
        hidden = (gate / (1.0 + jnp.exp(-gate)) * up).astype(BF16)
        result = jnp.dot(hidden, w[2], preferred_element_type=F32)
        row = 0
        for s, a, n in blocks:
            acc[s, a : a + n] = result[row : row + n]
            row += n

    def reduce(way, step, piece):
        at = pl.ds(piece * part, part)
        slot = 4 * step + far[way].index(piece) if piece in far[way] else 4 * step - 2 + near[way].index(piece)
        return pltpu.make_async_remote_copy(
            src_ref=sums.at[4 * way + step, at],
            dst_ref=came.at[4 * way + step, at],
            send_sem=rs_send,
            recv_sem=rs_recv.at[way, slot],
            device_id=towards[way],
            device_id_type=MESH,
        )

    def send_sum(step, which, i):
        for way in (UP, DOWN):
            piece = which[way][i]
            at = pl.ds(piece * part, part)
            value = acc[4 + step if way == UP else 4 - step, at]
            if step > 1 or (step == 1 and which is far):
                reduce(way, step - 1, piece).wait_recv()
                value = value + came[4 * way + step - 1, at].astype(F32)
            sums[4 * way + step, at] = value.astype(BF16)
            reduce(way, step, piece).start()

    pass_on(0, far, 0)
    pass_on(0, far, 1)
    pass_on(0, near, 0)
    pltpu.make_async_copy(own, own, w_load).wait()
    for i in range(3):
        from_partner(i).start()
    pass_on(1, far, 0)
    pass_on(1, far, 1)
    pass_on(0, near, 1)
    arrived_weights(0)
    pass_on(2, far, 0)
    pass_on(2, far, 1)
    pass_on(1, near, 0)
    arrived_weights(1)
    pass_on(3, far, 0)
    arrived_weights(2)
    pass_on(3, far, 1)
    pass_on(1, near, 1)
    for i in range(3):
        hand_on(i).wait_recv()
    work((3, half, half), (5, 0, half))
    pass_on(2, near, 0)
    send_sum(1, near, 0)
    work((0, 0, rows), (1, 0, rows), (7, 0, rows))
    for way in (UP, DOWN):
        for piece in far[way]:
            gather(way, 3, piece).wait_recv()
    work((4, 0, rows))
    pass_on(2, near, 1)
    send_sum(0, far, 0)
    send_sum(0, far, 1)
    send_sum(1, near, 1)
    work((2, 0, rows), (6, 0, rows))
    for way in (UP, DOWN):
        for piece in near[way]:
            gather(way, 2, piece).wait_recv()
    work((3, 0, half), (5, half, half))
    send_sum(1, far, 0)
    send_sum(1, far, 1)
    for step in (2, 3):
        for which in (near, far):
            for i in (0, 1):
                send_sum(step, which, i)
    for which in (near, far):
        for i in (0, 1):
            for way in (UP, DOWN):
                piece = which[way][i]
                at = pl.ds(piece * part, part)
                reduce(way, 3, piece).wait_recv()
                value = acc[0, at] + came[4 * way + 3, at].astype(F32)
                if which is near:
                    acc[0, at] = value
                else:
                    out_ref[at] = value.astype(BF16)

    for sent, sem in ((x.at[pl.ds(0, 7)], ag_send), (sums.at[pl.ds(0, 7)], rs_send), (own, w_send)):
        pltpu.make_async_copy(sent, sent, sem).wait()


def shards(tokens, smooth_scale, gate_weight, up_weight, down_weight):
    rows, width = tokens.shape
    units = gate_weight.shape[0]
    here = pl.BlockSpec(memory_space=pltpu.HBM)
    operands = (tokens, smooth_scale, gate_weight, up_weight, down_weight)
    dma = pltpu.SemaphoreType.DMA
    return pl.pallas_call(
        kernel,
        out_shape=pltpu.VMEM((rows, width), BF16),
        in_specs=[here] * 5,
        out_specs=pl.BlockSpec(memory_space=pltpu.VMEM),
        scratch_shapes=[
            pltpu.VMEM((rows, width), BF16),
            pltpu.VMEM((width,), F32),
            pltpu.VMEM((8, rows, width), BF16),
            pltpu.VMEM((3, 2 * units, width), BF16),
            pltpu.VMEM((8, rows, width), F32),
            pltpu.VMEM((8, rows, width), BF16),
            pltpu.VMEM((8, rows, width), BF16),
            dma((2,)),
            dma,
            dma((2, 14)),
            dma,
            dma((2, 14)),
            dma,
            dma,
            dma((3,)),
            dma((3,)),
        ],
        compiler_params=pltpu.CompilerParams(
            collective_id=0, has_side_effects=True, vmem_limit_bytes=48 << 20
        ),
    )(*(pltpu.with_memory_space_constraint(o, pltpu.HBM) for o in operands))


def solution(mesh):
    return jax.shard_map(
        shards,
        mesh=mesh,
        in_specs=(
            P(("dp", "tensor"), None),
            P(),
            P("tensor", None),
            P("tensor", None),
            P("tensor", None),
        ),
        out_specs=P(("dp", "tensor"), None),
        check_vma=False,
    )
```

time: 51.2 us -> 48.8 us (0.953)
  Pallas kernels: 50.1 us -> 47.9 us
    pallas_call x1, Pallas kernels: 50.1 us -> 47.9 us  [shards(): pl.pallas_call(kernel, out_shape=pltpu.VMEM((rows, width), BF16), in_spec...]
where the time goes in v4:
time: 48.8 us; the launch traced here: 48.5 us
  Pallas kernels  47.9 us (98%)
  local copies, waits for them, and re-layouts  0.69 us (1%)
    pallas_call x1, Pallas kernels, shards(): pl.pallas_call(kernel, out_shape=pltpu.VMEM((rows, width), BF16), in_spec...  47.9 us

profile of v4, /device:TPU:56, one launch (start us, length us, event | category | flops | bytes accessed | tf_op | source)
XLA Modules:
  0.0 48.5 jit_solution(6324329185129411318)
XLA Ops:
  0.0 47.9 %shard_map.55 = bf16[128,896]{1,0:T(8,128)(2,1)S(1)} custom-call(bf16[128,896]{1,0:T(8,128)(2,1)} %tokens_ref.1, f32[896]{0:T(1024)} %scale_ref.1, bf16[304,896]{1,0:T(8,128)(2,1)} %gate_ref.1, bf16[304,896]{1,0:T(8,128)(2,1)} %up_ref.1, bf16[304,896]{1,0:T(8,128)(2,1)} %down_ref.1), custom_call_target="tpu_custom_call" | custom-call | tf_op jit(solution)/shard_map/pallas_call | solution.py:200
  47.9 0.7 %copy.7 = bf16[128,896]{1,0:T(8,128)(2,1)} copy(bf16[128,896]{1,0:T(8,128)(2,1)S(1)} %shard_map.55) | data formatting | bytes 458752

commit v5 on v4

--- a/solution.py
+++ b/solution.py
@@ -15,14 +15,17 @@
 def kernel(
     tokens_ref, scale_ref, gate_ref, up_ref, down_ref, out_ref,
     raw, scale, x, w, acc, sums, came,
-    load_sem, ag_send, ag_recv, rs_send, rs_recv, w_load, w_send, w_recv, f_recv,
+    load_sem, ag_send, rs_send, recv, w_load, w_send, w_recv, f_recv,
 ):
     dp, t = lax.axis_index("dp"), lax.axis_index("tensor")
-    core, x_hi = lax.rem(dp, 2), lax.rem(dp // 2, 2)
-    other_t = t + 1 - 2 * lax.rem(t, 2)
-    towards = ((dp, lax.rem(t + 2, 16)), (dp, lax.rem(t + 14, 16)))
+    core, x_hi, x_lo = dp & 1, (dp >> 1) & 1, t & 1
+    other_t = t + 1 - 2 * x_lo
+    towards = ((dp, (t + 2) & 15), (dp, (t + 14) & 15))
     sibling = (dp + 1 - 2 * core, t)
     partner = (dp + core * (2 - 4 * x_hi), other_t)
+    barrier = pltpu.get_barrier_semaphore()
+    for device in (*towards, sibling, partner):
+        pl.semaphore_signal(barrier, inc=1, device_id=device, device_id_type=MESH)
 
     rows = tokens_ref.shape[0]
     part = rows // PIECES
@@ -31,21 +34,20 @@
     big = (units // 2 + 15) // 16 * 16
     small = units - big
 
+    own = w.at[:, pl.ds(0, units)]
     loads = [
-        pltpu.make_async_copy(scale_ref, scale, load_sem.at[0]),
-        pltpu.make_async_copy(tokens_ref, raw, load_sem.at[1]),
+        pltpu.make_async_copy(tokens_ref, raw, load_sem.at[0]),
+        pltpu.make_async_copy(scale_ref, scale, load_sem.at[1]),
     ]
-    for i, ref in enumerate((gate_ref, up_ref, down_ref)):
-        loads.append(pltpu.make_async_copy(ref, w.at[i, pl.ds(0, units)], w_load))
-    own = w.at[:, pl.ds(0, units)]
-    barrier = pltpu.get_barrier_semaphore()
-    for device in (*towards, sibling, partner):
-        pl.semaphore_signal(barrier, inc=1, device_id=device, device_id_type=MESH)
     for load in loads:
         load.start()
-    loads[0].wait()
-    loads[1].wait()
-    x[0] = (raw[...].astype(F32) / scale[...][None, :]).astype(BF16)
+
+    for load in loads:
+        load.wait()
+    for i, ref in enumerate((gate_ref, up_ref, down_ref)):
+        pltpu.make_async_copy(ref, w.at[i, pl.ds(0, units)], w_load).start()
+    inverse = 1.0 / scale[...][None, :]
+    x[0] = (raw[...].astype(F32) * inverse).astype(BF16)
     pl.semaphore_wait(barrier, 4)
 
     far = ((2, 3), (0, 1))
@@ -60,7 +62,7 @@
             src_ref=x.at[here, at],
             dst_ref=x.at[there, at],
             send_sem=ag_send,
-            recv_sem=ag_recv.at[way, slot],
+            recv_sem=recv.at[way, slot],
             device_id=towards[way],
             device_id_type=MESH,
         )
@@ -109,14 +111,17 @@
             acc[s, a : a + n] = result[row : row + n]
             row += n
 
+    takes_over = {(0, far): 4, (1, near): 0, (1, far): 2, (2, near): 8, (2, far): 6, (3, near): 10, (3, far): 12}
+
     def reduce(way, step, piece):
         at = pl.ds(piece * part, part)
-        slot = 4 * step + far[way].index(piece) if piece in far[way] else 4 * step - 2 + near[way].index(piece)
+        which = far if piece in far[way] else near
+        slot = takes_over[step, which] + which[way].index(piece)
         return pltpu.make_async_remote_copy(
             src_ref=sums.at[4 * way + step, at],
             dst_ref=came.at[4 * way + step, at],
             send_sem=rs_send,
-            recv_sem=rs_recv.at[way, slot],
+            recv_sem=recv.at[way, slot],
             device_id=towards[way],
             device_id_type=MESH,
         )
@@ -134,47 +139,52 @@
 
     pass_on(0, far, 0)
     pass_on(0, far, 1)
-    pass_on(0, near, 0)
     pltpu.make_async_copy(own, own, w_load).wait()
     for i in range(3):
         from_partner(i).start()
+    pass_on(0, near, 0)
+    pass_on(0, near, 1)
     pass_on(1, far, 0)
     pass_on(1, far, 1)
-    pass_on(0, near, 1)
+    pass_on(1, near, 0)
+    pass_on(2, far, 0)
     arrived_weights(0)
-    pass_on(2, far, 0)
     pass_on(2, far, 1)
-    pass_on(1, near, 0)
+    pass_on(1, near, 1)
     arrived_weights(1)
     pass_on(3, far, 0)
     arrived_weights(2)
     pass_on(3, far, 1)
-    pass_on(1, near, 1)
+    pass_on(2, near, 0)
     for i in range(3):
         hand_on(i).wait_recv()
     work((3, half, half), (5, 0, half))
-    pass_on(2, near, 0)
+    pass_on(2, near, 1)
+    work((1, 0, rows), (7, 0, rows))
     send_sum(1, near, 0)
-    work((0, 0, rows), (1, 0, rows), (7, 0, rows))
     for way in (UP, DOWN):
         for piece in far[way]:
             gather(way, 3, piece).wait_recv()
     work((4, 0, rows))
-    pass_on(2, near, 1)
+    send_sum(0, far, 1)
     send_sum(0, far, 0)
-    send_sum(0, far, 1)
+    work((2, 0, rows), (6, 0, rows))
     send_sum(1, near, 1)
-    work((2, 0, rows), (6, 0, rows))
     for way in (UP, DOWN):
         for piece in near[way]:
             gather(way, 2, piece).wait_recv()
     work((3, 0, half), (5, half, half))
+    send_sum(2, near, 0)
+    send_sum(1, far, 1)
     send_sum(1, far, 0)
-    send_sum(1, far, 1)
-    for step in (2, 3):
-        for which in (near, far):
-            for i in (0, 1):
-                send_sum(step, which, i)
+    work((0, 0, rows))
+    send_sum(2, near, 1)
+    send_sum(2, far, 1)
+    send_sum(2, far, 0)
+    send_sum(3, near, 1)
+    send_sum(3, near, 0)
+    send_sum(3, far, 1)
+    send_sum(3, far, 0)
     for which in (near, far):
         for i in (0, 1):
             for way in (UP, DOWN):
@@ -212,7 +222,6 @@
             pltpu.VMEM((8, rows, width), BF16),
             dma((2,)),
             dma,
-            dma((2, 14)),
             dma,
             dma((2, 14)),
             dma,

time: 48.8 us -> 48.4 us (level)
  no operation moved by 1% of the time
where the time goes in v5:
time: 48.4 us; the launch traced here: 48.3 us
  Pallas kernels  47.6 us (98%)
  local copies, waits for them, and re-layouts  0.69 us (1%)
    pallas_call x1, Pallas kernels, shards(): pl.pallas_call(kernel, out_shape=pltpu.VMEM((rows, width), BF16), in_spec...  47.6 us

profile of v5, /device:TPU:56, one launch (start us, length us, event | category | flops | bytes accessed | tf_op | source)
XLA Modules:
  0.0 48.3 jit_solution(7389809811757922290)
XLA Ops:
  0.0 47.6 %shard_map.55 = bf16[128,896]{1,0:T(8,128)(2,1)S(1)} custom-call(bf16[128,896]{1,0:T(8,128)(2,1)} %tokens_ref.1, f32[896]{0:T(1024)} %scale_ref.1, bf16[304,896]{1,0:T(8,128)(2,1)} %gate_ref.1, bf16[304,896]{1,0:T(8,128)(2,1)} %up_ref.1, bf16[304,896]{1,0:T(8,128)(2,1)} %down_ref.1), custom_call_target="tpu_custom_call" | custom-call | tf_op jit(solution)/shard_map/pallas_call | solution.py:210
  47.6 0.7 %copy.7 = bf16[128,896]{1,0:T(8,128)(2,1)} copy(bf16[128,896]{1,0:T(8,128)(2,1)S(1)} %shard_map.55) | data formatting | bytes 458752

commit v6 on v5

--- a/solution.py
+++ b/solution.py
@@ -9,7 +9,7 @@
 BF16, F32 = jnp.bfloat16, jnp.float32
 ROWS_BY_COLS = (((1,), (1,)), ((), ()))
 UP, DOWN = 0, 1
-PIECES = 4
+FAR_PIECES, NEAR_PIECES = 2, 2
 
 
 def kernel(
@@ -20,15 +20,13 @@
     dp, t = lax.axis_index("dp"), lax.axis_index("tensor")
     core, x_hi, x_lo = dp & 1, (dp >> 1) & 1, t & 1
     other_t = t + 1 - 2 * x_lo
-    towards = ((dp, (t + 2) & 15), (dp, (t + 14) & 15))
     sibling = (dp + 1 - 2 * core, t)
     partner = (dp + core * (2 - 4 * x_hi), other_t)
     barrier = pltpu.get_barrier_semaphore()
-    for device in (*towards, sibling, partner):
+    for device in (partner, (dp, (t + 2) & 15), (dp, (t + 14) & 15), sibling):
         pl.semaphore_signal(barrier, inc=1, device_id=device, device_id_type=MESH)
 
     rows = tokens_ref.shape[0]
-    part = rows // PIECES
     half = rows // 2
     units = gate_ref.shape[0]
     big = (units // 2 + 15) // 16 * 16
@@ -50,28 +48,36 @@
     x[0] = (raw[...].astype(F32) * inverse).astype(BF16)
     pl.semaphore_wait(barrier, 4)
 
-    far = ((2, 3), (0, 1))
-    near = ((0, 1), (2, 3))
-
-    def gather(way, hop, piece):
-        here = hop if way == UP else (8 - hop) % 8
-        there = hop + 1 if way == UP else 7 - hop
-        at = pl.ds(piece * part, part)
-        slot = 4 * hop + (far[way] + near[way]).index(piece)
+    ways = (UP, DOWN)
+    far, near = 0, 1
+
+    pieces = (FAR_PIECES, NEAR_PIECES)
+
+    def piece_at(way, which, i):
+        size = half // pieces[which]
+        return pl.ds(pl.multiple_of(i * size + half * (way if which == near else 1 - way), size), size)
+
+    def towards(way):
+        return (dp, (t + 2 + 12 * way) & 15)
+
+    def gather(way, hop, which, i):
+        here = hop + way * (8 - 2 * hop) if hop else 0
+        there = hop + 1 + way * (6 - 2 * hop)
+        at = piece_at(way, which, i)
         return pltpu.make_async_remote_copy(
             src_ref=x.at[here, at],
             dst_ref=x.at[there, at],
             send_sem=ag_send,
-            recv_sem=recv.at[way, slot],
-            device_id=towards[way],
+            recv_sem=recv.at[way, sum(pieces) * hop + which * FAR_PIECES + i],
+            device_id=towards(way),
             device_id_type=MESH,
         )
 
     def pass_on(hop, which, i):
-        for way in (UP, DOWN):
+        for way in ways:
             if hop:
-                gather(way, hop - 1, which[way][i]).wait_recv()
-            gather(way, hop, which[way][i]).start()
+                gather(way, hop - 1, which, i).wait_recv()
+            gather(way, hop, which, i).start()
 
     def from_partner(i):
         which, start, size = ((core, 0, big), (core, big, small), (2, core * small, big))[i]
@@ -111,31 +117,40 @@
             acc[s, a : a + n] = result[row : row + n]
             row += n
 
-    takes_over = {(0, far): 4, (1, near): 0, (1, far): 2, (2, near): 8, (2, far): 6, (3, near): 10, (3, far): 12}
-
-    def reduce(way, step, piece):
-        at = pl.ds(piece * part, part)
-        which = far if piece in far[way] else near
-        slot = takes_over[step, which] + which[way].index(piece)
+    def slots(hop, which):
+        start = sum(pieces) * hop + which * FAR_PIECES
+        return list(range(start, start + pieces[which]))
+
+    takes_over = {
+        (0, far): slots(1, far),
+        (1, near): slots(0, far)[:NEAR_PIECES],
+        (1, far): slots(0, far)[NEAR_PIECES:] + slots(0, near),
+        (2, near): slots(2, far)[:NEAR_PIECES],
+        (2, far): slots(2, far)[NEAR_PIECES:] + slots(1, near),
+        (3, near): slots(2, near),
+        (3, far): slots(3, far),
+    }
+
+    def reduce(way, step, which, i):
+        at = piece_at(way, which, i)
         return pltpu.make_async_remote_copy(
             src_ref=sums.at[4 * way + step, at],
             dst_ref=came.at[4 * way + step, at],
             send_sem=rs_send,
-            recv_sem=recv.at[way, slot],
-            device_id=towards[way],
+            recv_sem=recv.at[way, takes_over[step, which][i]],
+            device_id=towards(way),
             device_id_type=MESH,
         )
 
     def send_sum(step, which, i):
-        for way in (UP, DOWN):
-            piece = which[way][i]
-            at = pl.ds(piece * part, part)
-            value = acc[4 + step if way == UP else 4 - step, at]
-            if step > 1 or (step == 1 and which is far):
-                reduce(way, step - 1, piece).wait_recv()
+        for way in ways:
+            at = piece_at(way, which, i)
+            value = acc[4 + step - 2 * step * way, at]
+            if step > 1 or (step == 1 and which == far):
+                reduce(way, step - 1, which, i).wait_recv()
                 value = value + came[4 * way + step - 1, at].astype(F32)
             sums[4 * way + step, at] = value.astype(BF16)
-            reduce(way, step, piece).start()
+            reduce(way, step, which, i).start()
 
     pass_on(0, far, 0)
     pass_on(0, far, 1)
@@ -162,17 +177,17 @@
     pass_on(2, near, 1)
     work((1, 0, rows), (7, 0, rows))
     send_sum(1, near, 0)
-    for way in (UP, DOWN):
-        for piece in far[way]:
-            gather(way, 3, piece).wait_recv()
+    for i in range(FAR_PIECES):
+        for way in ways:
+            gather(way, 3, far, i).wait_recv()
     work((4, 0, rows))
     send_sum(0, far, 1)
     send_sum(0, far, 0)
     work((2, 0, rows), (6, 0, rows))
     send_sum(1, near, 1)
-    for way in (UP, DOWN):
-        for piece in near[way]:
-            gather(way, 2, piece).wait_recv()
+    for i in range(NEAR_PIECES):
+        for way in ways:
+            gather(way, 2, near, i).wait_recv()
     work((3, 0, half), (5, half, half))
     send_sum(2, near, 0)
     send_sum(1, far, 1)
@@ -181,18 +196,17 @@
     send_sum(2, near, 1)
     send_sum(2, far, 1)
     send_sum(2, far, 0)
+    send_sum(3, near, 0)
     send_sum(3, near, 1)
-    send_sum(3, near, 0)
     send_sum(3, far, 1)
     send_sum(3, far, 0)
     for which in (near, far):
-        for i in (0, 1):
-            for way in (UP, DOWN):
-                piece = which[way][i]
-                at = pl.ds(piece * part, part)
-                reduce(way, 3, piece).wait_recv()
+        for i in range(pieces[which]):
+            for way in ways:
+                at = piece_at(way, which, i)
+                reduce(way, 3, which, i).wait_recv()
                 value = acc[0, at] + came[4 * way + 3, at].astype(F32)
-                if which is near:
+                if which == near:
                     acc[0, at] = value
                 else:
                     out_ref[at] = value.astype(BF16)
@@ -223,7 +237,7 @@
             dma((2,)),
             dma,
             dma,
-            dma((2, 14)),
+            dma((2, 4 * FAR_PIECES + 3 * NEAR_PIECES)),
             dma,
             dma,
             dma((3,)),

time: 48.4 us -> 48.4 us (level)
  no operation moved by 1% of the time
where the time goes in v6:
time: 48.4 us; the launch traced here: 48.3 us
  Pallas kernels  47.6 us (98%)
  local copies, waits for them, and re-layouts  0.69 us (1%)
    pallas_call x1, Pallas kernels, shards(): pl.pallas_call(kernel, out_shape=pltpu.VMEM((rows, width), BF16), in_spec...  47.6 us

profile of v6, /device:TPU:56, one launch (start us, length us, event | category | flops | bytes accessed | tf_op | source)
XLA Modules:
  0.0 48.3 jit_solution(16751719174548739007)
XLA Ops:
  0.0 47.6 %shard_map.55 = bf16[128,896]{1,0:T(8,128)(2,1)S(1)} custom-call(bf16[128,896]{1,0:T(8,128)(2,1)} %tokens_ref.1, f32[896]{0:T(1024)} %scale_ref.1, bf16[304,896]{1,0:T(8,128)(2,1)} %gate_ref.1, bf16[304,896]{1,0:T(8,128)(2,1)} %up_ref.1, bf16[304,896]{1,0:T(8,128)(2,1)} %down_ref.1), custom_call_target="tpu_custom_call" | custom-call | tf_op jit(solution)/shard_map/pallas_call | solution.py:224
  47.6 0.7 %copy.7 = bf16[128,896]{1,0:T(8,128)(2,1)} copy(bf16[128,896]{1,0:T(8,128)(2,1)S(1)} %shard_map.55) | data formatting | bytes 458752

commit v7 on v6

--- a/solution.py
+++ b/solution.py
@@ -192,7 +192,6 @@
     send_sum(2, near, 0)
     send_sum(1, far, 1)
     send_sum(1, far, 0)
-    work((0, 0, rows))
     send_sum(2, near, 1)
     send_sum(2, far, 1)
     send_sum(2, far, 0)
@@ -200,6 +199,7 @@
     send_sum(3, near, 1)
     send_sum(3, far, 1)
     send_sum(3, far, 0)
+    work((0, 0, rows))
     for which in (near, far):
         for i in range(pieces[which]):
             for way in ways:

time: 48.4 us -> 48.4 us (level)
  no operation moved by 1% of the time
where the time goes in v7:
time: 48.4 us; the launch traced here: 48.3 us
  Pallas kernels  47.6 us (98%)
  local copies, waits for them, and re-layouts  0.69 us (1%)
    pallas_call x1, Pallas kernels, shards(): pl.pallas_call(kernel, out_shape=pltpu.VMEM((rows, width), BF16), in_spec...  47.6 us

profile of v7, /device:TPU:56, one launch (start us, length us, event | category | flops | bytes accessed | tf_op | source)
XLA Modules:
  0.0 48.3 jit_solution(3373694120368778457)
XLA Ops:
  0.0 47.6 %shard_map.55 = bf16[128,896]{1,0:T(8,128)(2,1)S(1)} custom-call(bf16[128,896]{1,0:T(8,128)(2,1)} %tokens_ref.1, f32[896]{0:T(1024)} %scale_ref.1, bf16[304,896]{1,0:T(8,128)(2,1)} %gate_ref.1, bf16[304,896]{1,0:T(8,128)(2,1)} %up_ref.1, bf16[304,896]{1,0:T(8,128)(2,1)} %down_ref.1), custom_call_target="tpu_custom_call" | custom-call | tf_op jit(solution)/shard_map/pallas_call | solution.py:224
  47.6 0.7 %copy.7 = bf16[128,896]{1,0:T(8,128)(2,1)} copy(bf16[128,896]{1,0:T(8,128)(2,1)S(1)} %shard_map.55) | data formatting | bytes 458752

commit v8 on v7

--- a/solution.py
+++ b/solution.py
@@ -154,11 +154,11 @@
 
     pass_on(0, far, 0)
     pass_on(0, far, 1)
+    pass_on(0, near, 0)
+    pass_on(0, near, 1)
     pltpu.make_async_copy(own, own, w_load).wait()
     for i in range(3):
         from_partner(i).start()
-    pass_on(0, near, 0)
-    pass_on(0, near, 1)
     pass_on(1, far, 0)
     pass_on(1, far, 1)
     pass_on(1, near, 0)

time: 48.4 us -> 48.4 us (level)
  no operation moved by 1% of the time
where the time goes in v8:
time: 48.4 us; the launch traced here: 48.3 us
  Pallas kernels  47.6 us (98%)
  local copies, waits for them, and re-layouts  0.69 us (1%)
    pallas_call x1, Pallas kernels, shards(): pl.pallas_call(kernel, out_shape=pltpu.VMEM((rows, width), BF16), in_spec...  47.6 us

profile of v8, /device:TPU:56, one launch (start us, length us, event | category | flops | bytes accessed | tf_op | source)
XLA Modules:
  0.0 48.3 jit_solution(4104018950179460001)
XLA Ops:
  0.0 47.6 %shard_map.55 = bf16[128,896]{1,0:T(8,128)(2,1)S(1)} custom-call(bf16[128,896]{1,0:T(8,128)(2,1)} %tokens_ref.1, f32[896]{0:T(1024)} %scale_ref.1, bf16[304,896]{1,0:T(8,128)(2,1)} %gate_ref.1, bf16[304,896]{1,0:T(8,128)(2,1)} %up_ref.1, bf16[304,896]{1,0:T(8,128)(2,1)} %down_ref.1), custom_call_target="tpu_custom_call" | custom-call | tf_op jit(solution)/shard_map/pallas_call | solution.py:224
  47.6 0.7 %copy.7 = bf16[128,896]{1,0:T(8,128)(2,1)} copy(bf16[128,896]{1,0:T(8,128)(2,1)S(1)} %shard_map.55) | data formatting | bytes 458752
